TPU v7x, 32 devices: a whole 2x2x4 slice. The times are simulated.
32 devices in a mesh: grp: 2 (over y), dp: 4 (over z), test: 2 (over x), seq: 2 (over core).
Axes of the slice: x: 2, y: 2, z: 4, core: 2. Of those that a mesh axis runs over, the one named last changes fastest.
Arguments:
- train_inputs: bfloat16 [16, 256, 4096], P(('grp', 'dp', 'test'), 'seq'), parts along dimension 0, may hold values from -48 to 48
- train_grads: bfloat16 [16, 256, 7168], P(('grp', 'dp', 'test'), 'seq'), parts along dimension 0, may hold values from -48 to 48
- lengths: int32 [16], P(('grp', 'dp', 'test')), parts along dimension 0, may hold values from 64 to 256, as said below
- proj_in: bfloat16 [64, 4096], replicated, may hold values from -4 to 4
- proj_out: bfloat16 [64, 7168], replicated, may hold values from -4 to 4
- test_grads: float32 [32, 4096], P(('grp', 'dp', 'test')), parts along dimension 0, may hold values from -0.03 to 0.03
Outputs:
- scores: float32 [32, 8], P(('grp', 'dp', 'test')), parts along dimension 0
There are 2 independent parts, one for each index of `grp`. A program takes and returns all parts, laid end to end along the dimension named above; an argument that names none is the same for every part. Nothing has to cross between parts.
Inputs may be any that keep to these rules, and one draw needn't show every extreme that they name: Sequence s holds real tokens in its first lengths[s] slots; some sequence is full.
All inputs are finite; a program needn't handle non-finite values.
Results may differ from a plain program's by a relative error of at most 0.0003.
Values sent between devices are 32-bit elements; how exact they have to be, the bound alone decides.
A program may use at most 64 MiB of HBM per device.

v0:
```python
import jax
import jax.numpy as jnp
from jax import lax
from jax.sharding import PartitionSpec as P

damping = 0.1


def damped_inverse(covariance, token_count):
    width = covariance.shape[0]
    normed = covariance / token_count
    shift = damping * jnp.trace(normed) / width
    damped = normed + shift * jnp.eye(width, dtype=jnp.float32)
    factor = jnp.linalg.cholesky(damped)
    return jax.scipy.linalg.cho_solve((factor, True), jnp.eye(width, dtype=jnp.float32))


def precondition(inv_out, matrices, inv_in):
    highest = lax.Precision.HIGHEST
    return jnp.matmul(jnp.matmul(inv_out, matrices, precision=highest), inv_in, precision=highest)


def per_device(train_inputs, train_grads, lengths, proj_in, proj_out, test_grads):
    highest = lax.Precision.HIGHEST
    seq_local, half_len, _ = train_inputs.shape
    out_width = proj_out.shape[0]
    in_width = proj_in.shape[0]
    first_slot = lax.axis_index("seq") * half_len
    positions = first_slot + jnp.arange(half_len, dtype=jnp.int32)
    valid_mask = (positions[None, :] < lengths[:, None]).astype(jnp.float32)
    inputs_low = (
        jnp.einsum("kd,std->skt", proj_in, train_inputs, preferred_element_type=jnp.float32)
        * valid_mask[:, None, :]
    )
    grads_low = (
        jnp.einsum("kd,std->skt", proj_out, train_grads, preferred_element_type=jnp.float32)
        * valid_mask[:, None, :]
    )
    partial_grad = jnp.einsum("sot,sit->soi", grads_low, inputs_low, precision=highest)
    cov_in_part = jnp.einsum("sit,sjt->ij", inputs_low, inputs_low, precision=highest)
    cov_out_part = jnp.einsum("sot,spt->op", grads_low, grads_low, precision=highest)
    count_part = jnp.sum(valid_mask)
    example_grad = lax.psum(partial_grad, "seq")
    cov_in, cov_out, token_count = lax.psum(
        (cov_in_part, cov_out_part, count_part), ("dp", "test", "seq")
    )
    inv_in = damped_inverse(cov_in, token_count)
    inv_out = damped_inverse(cov_out, token_count)
    test_local = test_grads.shape[0]
    test_mats = test_grads.reshape(test_local, out_width, in_width)
    test_side = precondition(inv_out, test_mats, inv_in).reshape(test_local, out_width * in_width)
    train_side = example_grad.reshape(seq_local, out_width * in_width)
    return jnp.dot(
        test_side,
        lax.all_gather(train_side, ("dp", "test"), axis=0, tiled=True).T,
        precision=highest,
    )


def solution(mesh):
    return jax.shard_map(
        per_device,
        mesh=mesh,
        in_specs=(
            P(("grp", "dp", "test"), "seq", None),
            P(("grp", "dp", "test"), "seq", None),
            P(("grp", "dp", "test")),
            P(),
            P(),
            P(("grp", "dp", "test"), None),
        ),
        out_specs=P(("grp", "dp", "test"), None),
        check_vma=False,
    )
```

profile of v0, /device:TPU:0, one launch (start us, length us, event | category | flops | bytes accessed | tf_op | source)
XLA Modules:
  0.0 136.6 jit_solution(14644721336629863902)
XLA Ops:
  0.8 0.7 fusion.29
  1.5 1.8 %fusion.3 = f32[64,128]{1,0:T(8,128)S(1)} fusion(bf16[64,4096]{1,0:T(8,128)(2,1)} %param.12, bf16[1,128,4096]{2,1,0:T(8,128)(2,1)} %param.9, f32[128]{0:T(128)S(1)} %get-tuple-element.11), kind=kOutput, calls=%fused_computation.5 | convolution fusion | flops 67117056 | bytes 1606144 | tf_op jit(solution)/shard_map/kd,std->skt/dot_general | solution.py:32
  3.3 1.9 %fusion.10 = f32[64,128]{1,0:T(8,128)S(1)} fusion(bf16[64,7168]{1,0:T(8,128)(2,1)} %param.13, bf16[1,128,7168]{2,1,0:T(8,128)(2,1)S(1)} %copy-done, f32[128]{0:T(128)S(1)} %get-tuple-element.11), kind=kOutput, calls=%fused_computation.10 | convolution fusion | flops 117448704 | bytes 2785792 | tf_op jit(solution)/shard_map/kd,std->skt/dot_general | solution.py:36
  5.3 0.2 fusion.33
  5.6 3.6 %psum.31 = f32[1,4096]{1,0:T(1,128)S(1)} all-reduce(f32[1,4096]{1,0:T(1,128)S(1)} %reshape.58), channel_id=1, replica_groups=mesh['grp'=2,'dp'=4,'test'=2,'seq'=2] {'seq'}, use_global_device_ids=true, to_apply=%region_8.11 | all-reduce | flops 4096 | bytes 32768 | tf_op jit(solution)/shard_map/psum | solution.py:43
  9.4 0.2 fusion.30
  9.6 65.0 %all-reduce = (f32[64,64]{0,1:T(8,128)S(1)}, f32[]{:T(128)}, f32[64,64]{0,1:T(8,128)S(1)}) all-reduce(f32[64,64]{0,1:T(8,128)S(1)} %fusion.30, f32[]{:T(128)} %get-tuple-element.10, f32[64,64]{0,1:T(8,128)S(1)} %fusion.31), channel_id=1, replica_groups=mesh['grp'=2,'dp'=4,'test'=2,'seq'=2] {'dp','test','seq'}, use_global_device_ids=true, to_apply=%region_0.0 | all-reduce | flops 8193 | bytes 65544 | tf_op jit(solution)/shard_map/psum | solution.py:44
  74.6 1.3 select_reduce_fusion.2
  76.6 1.3 select_reduce_fusion.3
  78.6 0.7 select_add_fusion
  79.4 5.8 %cholesky.55 = f32[64,64]{1,0:T(8,128)S(1)} custom-call(f32[64,64]{1,0:T(8,128)S(1)} %fusion.25), custom_call_target="Cholesky" | custom-call | tf_op jit(solution)/shard_map/jit(cholesky)/cholesky | solution.py:14
  85.3 0.6 compare_reduce_fusion
  85.9 0.7 fusion.22
  86.6 4.9 %custom-call.9 = f32[1,64,64]{1,2,0:T(8,128)S(1)} custom-call(f32[1,64,64]{2,1,0:T(8,128)S(1)} %fusion.22), custom_call_target="InvertDiagBlocksLowerTriangular" | custom-call | tf_op jit(solution)/shard_map/jit(_cho_solve)/triangular_solve | solution.py:15
  91.5 0.3 fusion.17
  92.0 5.8 %cholesky.44 = f32[64,64]{1,0:T(8,128)S(1)} custom-call(f32[64,64]{1,0:T(8,128)S(1)} %fusion.28), custom_call_target="Cholesky" | custom-call | tf_op jit(solution)/shard_map/jit(cholesky)/cholesky | solution.py:14
  97.9 0.6 compare_reduce_fusion.1
  98.5 0.7 fusion.21
  99.2 4.9 %custom-call.8 = f32[1,64,64]{1,2,0:T(8,128)S(1)} custom-call(f32[1,64,64]{2,1,0:T(8,128)S(1)} %fusion.21), custom_call_target="InvertDiagBlocksLowerTriangular" | custom-call | tf_op jit(solution)/shard_map/jit(_cho_solve)/triangular_solve | solution.py:15
  104.1 0.3 fusion.19
  104.6 0.2 convolution_bitcast_fusion
  104.8 0.2 fusion.32
  105.1 30.5 %all-gather = f32[8,1,4096]{2,1,0:T(1,128)S(1)} all-gather(f32[1,1,4096]{2,1,0:T(1,128)S(1)} %bitcast.81), channel_id=1, replica_groups=mesh['grp'=2,'dp'=4,'test'=2,'seq'=2] {'dp','test'}, dimensions={0}, use_global_device_ids=true | all-gather | bytes 147456 | tf_op jit(solution)/shard_map/all_gather | solution.py:55
  135.6 1.0 fusion.14
  (16 shorter events, 1.0 us)
Async XLA Ops:
  0.0 3.3 %copy-start = (bf16[1,128,7168]{2,1,0:T(8,128)(2,1)S(1)}, bf16[1,128,7168]{2,1,0:T(8,128)(2,1)}, u32[]{:S(2)}) copy-start(bf16[1,128,7168]{2,1,0:T(8,128)(2,1)} %param.10) | copy-start | bytes 5505028
  3.3 101.2 %copy-start.1 = (f32[2,4096]{1,0:T(2,128)S(1)}, f32[2,4096]{1,0:T(2,128)}, u32[]{:S(2)}) copy-start(f32[2,4096]{1,0:T(2,128)} %param.14) | copy-start | bytes 98308
where the time goes:
time: 137 us
  blocking collectives  99.1 us (72%)
  other arithmetic  28.2 us (21%)
  matrix products  6.51 us (5%)
  between operations  2.35 us (2%)
    psum x1, blocking collectives, per_device(): lax.psum((cov_in_part, cov_out_part, count_part), ('dp', 'test', 'seq'))  65 us
    all_gather x1, blocking collectives, per_device(): lax.all_gather(train_side, ('dp', 'test'), axis=0, tiled=True)  30.5 us
    another operation x6, other arithmetic, damped_inverse(): factor = jnp.linalg.cholesky(damped)  13 us
    another operation x4, other arithmetic, damped_inverse(): jax.scipy.linalg.cho_solve((factor, True), jnp.eye(width, dtype=jnp.float...  11.1 us
    psum x1, blocking collectives, per_device(): example_grad = lax.psum(partial_grad, 'seq')  3.64 us

commit v1 on v0

v1 whole, which is shorter than its diff:
```python
import functools

import jax
import jax.numpy as jnp
from jax import lax
from jax.experimental import pallas as pl
from jax.experimental.pallas import tpu as pltpu
from jax.sharding import PartitionSpec as P

damping = 0.1
HIGHEST = lax.Precision.HIGHEST
F32 = jnp.float32


def dot_nt(a, b, precision=None):
    return lax.dot_general(
        a, b, (((1,), (1,)), ((), ())), precision=precision, preferred_element_type=F32
    )


def dot_nn(a, b):
    return jnp.dot(a, b, precision=HIGHEST, preferred_element_type=F32)


def chunk_of(width):
    for size in (1024, 512, 256, 128):
        if width % size == 0:
            return size
    return width


def twin_inverse(tiles, width):
    wide = tiles[0].shape[1]
    lane = lax.rem(lax.broadcasted_iota(jnp.int32, (8, wide), 1), width)
    row = lax.broadcasted_iota(jnp.int32, (8, wide), 0)
    tiles = list(tiles)
    count = width // 8
    for k in range(count):
        inside = (lane >= 8 * k) & (lane < 8 * k + 8)
        pivots = tiles[k]
        cols = [jnp.broadcast_to(pivots[:, 8 * k + j : 8 * k + j + 1], (8, wide)) for j in range(8)]
        work = jnp.where(inside, (lane - 8 * k == row).astype(F32), pivots)
        for j in range(8):
            scale = 1.0 / cols[j][j : j + 1, :]
            here = row == j
            factor = cols[j]
            line = work[j : j + 1, :] * scale
            work = jnp.where(here, line, work - factor * line)
            for m in range(j + 1, 8):
                line = cols[m][j : j + 1, :] * scale
                cols[m] = jnp.where(here, line, cols[m] - factor * line)
        for i in range(count):
            if i == k:
                continue
            total = jnp.where(inside, 0.0, tiles[i])
            for j in range(8):
                column = jnp.broadcast_to(
                    tiles[i][:, 8 * k + j : 8 * k + j + 1], (8, wide)
                )
                total = total - column * work[j : j + 1, :]
            tiles[i] = total
        tiles[k] = work
    return tiles


def kernel(
    n_dp, n_test,
    lengths_ref, tests_ref, xin_hbm, xout_hbm, pin_hbm, pout_hbm, out_ref,
    xin, xout, pin, pout, gram, sbuf, xbuf, zbuf, gbuf, tmat, inv_own, inv_other,
    load_sem, s_send, s_recv, x_send, x_recv, z_send, z_recv, g_send, g_recv, i_send, i_recv,
):
    dp = lax.axis_index("dp")
    test = lax.axis_index("test")
    core = lax.axis_index("seq")
    half_len, depth_in = xin.shape
    depth_out = xout.shape[1]
    width = pin.shape[0]
    test_local = tests_ref.shape[0]
    wide = 2 * width
    half = width // 2
    pairs = n_test // 2

    partners = [{"seq": 1 - core}]
    partners += [{"test": lax.rem(test + d, n_test)} for d in range(1, n_test)]
    partners += [{"dp": lax.rem(dp + d, n_dp)} for d in range(1, n_dp)]

    barrier = pltpu.get_barrier_semaphore()
    for partner in partners:
        pl.semaphore_signal(barrier, inc=1, device_id=partner, device_id_type=pl.DeviceIdType.MESH)

    loads = []
    plan = []
    for x_hbm, x, p_hbm, p, depth in (
        (xin_hbm, xin, pin_hbm, pin, depth_in),
        (xout_hbm, xout, pout_hbm, pout, depth_out),
    ):
        size = chunk_of(depth)
        steps = []
        for start in range(0, depth, size):
            cut = pl.ds(start, size)
            both = []
            for src, dst in ((x_hbm.at[0, :, cut], x.at[:, cut]), (p_hbm.at[:, cut], p.at[:, cut])):
                copy = pltpu.make_async_copy(src, dst, load_sem.at[len(loads)])
                copy.start()
                loads.append(copy)
                both.append(copy)
            steps.append((start, size, both))
        plan.append((x, p, steps))

    for j in range(test_local):
        for q in range(width * width // wide):
            piece = tests_ref[j : j + 1, q * wide : (q + 1) * wide]
            tmat[j, 2 * q : 2 * q + 1, :] = piece
            tmat[j, 2 * q + 1 : 2 * q + 2, :] = pltpu.roll(piece, width, 1)

    length = lengths_ref[0]
    slots = core * half_len + lax.broadcasted_iota(jnp.int32, (1, half_len), 1)
    valid = (slots < length).astype(F32)
    lows = []
    for x, p, steps in plan:
        total = jnp.zeros((width, half_len), F32)
        for start, size, both in steps:
            for copy in both:
                copy.wait()
            total = total + dot_nt(p[:, start : start + size], x[:, start : start + size])
        lows.append(total * valid)
    low_in, low_out = lows
    own = jnp.where(core == 0, low_in, low_out)
    oth = jnp.where(core == 0, low_out, low_in)

    pl.semaphore_wait(barrier, len(partners))

    gram[...] = dot_nt(oth, jnp.concatenate([oth, own], axis=0), HIGHEST)
    s_copy = pltpu.make_async_remote_copy(
        gram, sbuf, s_send, s_recv, device_id={"seq": 1 - core},
        device_id_type=pl.DeviceIdType.MESH,
    )
    s_copy.start()
    mine = dot_nt(own, jnp.concatenate([own, oth], axis=0), HIGHEST)
    tokens = jnp.clip(length, 0, 2 * half_len).astype(F32)
    xbuf[test, width : width + 8, :] = jnp.full((8, wide), tokens, F32)
    s_copy.wait_recv()
    xbuf[test, 0:width, :] = mine + sbuf[...]

    waits = [s_copy]

    def spread(buffer, me, axis, n, send, recv):
        arrivals = []
        for d in range(1, n):
            copy = pltpu.make_async_remote_copy(
                buffer.at[me], buffer.at[me], send.at[d - 1], recv.at[d - 1],
                device_id={axis: lax.rem(me + d, n)}, device_id_type=pl.DeviceIdType.MESH,
            )
            copy.start()
            waits.append(copy)
            source = lax.rem(me + n - d, n)
            arrivals.append(
                pltpu.make_async_remote_copy(
                    buffer.at[source], buffer.at[source], send.at[d - 1], recv.at[d - 1],
                    device_id={axis: lax.rem(me + d, n)}, device_id_type=pl.DeviceIdType.MESH,
                )
            )
        return arrivals

    for arrival in spread(xbuf, test, "test", n_test, x_send, x_recv):
        arrival.wait_recv()
    lane = lax.broadcasted_iota(jnp.int32, (half, wide), 1)
    left = lane < width
    cov = xbuf[0, 0:width, :]
    for i in range(1, n_test):
        cov = cov + xbuf[i, 0:width, :]
    zbuf[dp] = jnp.where(left, cov[0:half], pltpu.roll(cov[half:width], width, 1))
    z_arrivals = spread(zbuf, dp, "dp", n_dp, z_send, z_recv)
    left_full = lax.broadcasted_iota(jnp.int32, (width, wide), 1) < width
    for i in range(pairs):
        gbuf[dp, i * width : (i + 1) * width, :] = jnp.where(
            left_full,
            pltpu.roll(xbuf[2 * i, 0:width, :], width, 1),
            xbuf[2 * i + 1, 0:width, :],
        )
    amount = xbuf[0, width : width + 8, :]
    for i in range(1, n_test):
        amount = amount + xbuf[i, width : width + 8, :]
    gbuf[dp, pairs * width : pairs * width + 8, :] = amount
    g_arrivals = spread(gbuf, dp, "dp", n_dp, g_send, g_recv)

    for arrival in z_arrivals:
        arrival.wait_recv()
    packed = zbuf[0]
    for i in range(1, n_dp):
        packed = packed + zbuf[i]
    turned = pltpu.roll(packed, width, 1)
    twin = jnp.concatenate(
        [jnp.where(left, packed, turned), jnp.where(left, turned, packed)], axis=0
    )
    eye = lax.broadcasted_iota(jnp.int32, (width, wide), 0) == lax.rem(
        lax.broadcasted_iota(jnp.int32, (width, wide), 1), width
    )
    diagonal = jnp.where(eye, twin, 0.0)
    shift = (damping / width) * (0.5 * jnp.sum(diagonal))
    damped = twin + jnp.where(eye, shift, 0.0)
    tiles = twin_inverse([damped[8 * i : 8 * i + 8] for i in range(width // 8)], width)
    inverse = jnp.concatenate(tiles, axis=0)
    inv_own[...] = inverse
    i_copy = pltpu.make_async_remote_copy(
        inv_own, inv_other, i_send, i_recv, device_id={"seq": 1 - core},
        device_id_type=pl.DeviceIdType.MESH,
    )
    i_copy.start()
    waits.append(i_copy)

    sides = []
    for j in range(test_local):
        matrix = tmat[j][:, 0:width]
        sides.append(dot_nn(inverse[:, 0:width], jnp.where(core == 0, matrix.T, matrix)))
    sides = jnp.concatenate(sides, axis=0)
    for arrival in g_arrivals:
        arrival.wait_recv()
    amount = gbuf[0, pairs * width : pairs * width + 1, :]
    for i in range(1, n_dp):
        amount = amount + gbuf[i, pairs * width : pairs * width + 1, :]
    i_copy.wait_recv()
    scorer = dot_nn(sides, inv_other[...])
    left_row = lax.broadcasted_iota(jnp.int32, (1, wide), 1) < width
    ones = jnp.ones((8, wide), F32)
    for j in range(test_local):
        rows = []
        for z in range(n_dp):
            for i in range(pairs):
                part = jnp.sum(
                    scorer[j * width : (j + 1) * width] * gbuf[z, i * width : (i + 1) * width, :],
                    axis=0, keepdims=True,
                )
                part = part * amount * amount
                rows.append(jnp.where(left_row, part, 0.0))
                rows.append(jnp.where(left_row, 0.0, part))
        result = dot_nt(ones, jnp.concatenate(rows, axis=0), HIGHEST)
        out_ref[j : j + 1, :] = result[0:1, :]

    for copy in waits:
        copy.wait_send()


def per_device(n_dp, n_test, train_inputs, train_grads, lengths, proj_in, proj_out, test_grads):
    _, half_len, depth_in = train_inputs.shape
    depth_out = train_grads.shape[2]
    width = proj_in.shape[0]
    wide = 2 * width
    test_local = test_grads.shape[0]
    bf16 = train_inputs.dtype
    n_loads = 2 * (depth_in // chunk_of(depth_in) + depth_out // chunk_of(depth_out))
    any_space = pl.BlockSpec(memory_space=pl.ANY)
    dma = pltpu.SemaphoreType.DMA
    return pl.pallas_call(
        functools.partial(kernel, n_dp, n_test),
        out_shape=jax.ShapeDtypeStruct((test_local, n_dp * n_test), F32),
        in_specs=[
            pl.BlockSpec(memory_space=pltpu.SMEM),
            pl.BlockSpec(memory_space=pltpu.VMEM),
            any_space, any_space, any_space, any_space,
        ],
        out_specs=pl.BlockSpec(memory_space=pltpu.VMEM),
        scratch_shapes=[
            pltpu.VMEM((half_len, depth_in), bf16),
            pltpu.VMEM((half_len, depth_out), bf16),
            pltpu.VMEM((width, depth_in), bf16),
            pltpu.VMEM((width, depth_out), bf16),
            pltpu.VMEM((width, wide), F32),
            pltpu.VMEM((width, wide), F32),
            pltpu.VMEM((n_test, width + 8, wide), F32),
            pltpu.VMEM((n_dp, width // 2, wide), F32),
            pltpu.VMEM((n_dp, n_test // 2 * width + 8, wide), F32),
            pltpu.VMEM((test_local, width, wide), F32),
            pltpu.VMEM((width, wide), F32),
            pltpu.VMEM((width, wide), F32),
            dma((n_loads,)),
            dma, dma,
            dma((n_test - 1,)), dma((n_test - 1,)),
            dma((n_dp - 1,)), dma((n_dp - 1,)),
            dma((n_dp - 1,)), dma((n_dp - 1,)),
            dma, dma,
        ],
        compiler_params=pltpu.CompilerParams(
            collective_id=0, has_side_effects=True, vmem_limit_bytes=32 * 1024 * 1024
        ),
    )(lengths, test_grads, train_inputs, train_grads, proj_in, proj_out)


def solution(mesh):
    return jax.shard_map(
        functools.partial(per_device, mesh.shape["dp"], mesh.shape["test"]),
        mesh=mesh,
        in_specs=(
            P(("grp", "dp", "test"), "seq", None),
            P(("grp", "dp", "test"), "seq", None),
            P(("grp", "dp", "test")),
            P(),
            P(),
            P(("grp", "dp", "test"), None),
        ),
        out_specs=P(("grp", "dp", "test"), None),
        check_vma=False,
    )
```

time: 137 us -> 25.2 us (0.18)
  the two profiles are of different devices: /device:TPU:0 before, /device:TPU:1 now
where the time goes in v1:
time: 25.2 us; the launch traced here: 24.9 us
  Pallas kernels  18 us (71%)
  local copies, waits for them, and re-layouts  6.26 us (25%)
  between operations  0.67 us (3%)
    pallas_call x1, Pallas kernels, per_device(): pl.pallas_call(functools.partial(kernel, n_dp, n_test), out_shape=jax.Sha...  18 us
    unnamed x11, local copies, waits for them, and re-layouts  6.26 us

profile of v1, /device:TPU:1, one launch (start us, length us, event | category | flops | bytes accessed | tf_op | source)
XLA Modules:
  0.0 24.9 jit_solution(2530334843173737632)
XLA Ops:
  0.7 0.0 copy-start
  0.7 1.5 %copy-done = bf16[1,128,7168]{2,1,0:T(8,128)(2,1)S(1)} copy-done((bf16[1,128,7168]{2,1,0:T(8,128)(2,1)S(1)}, bf16[1,128,7168]{2,1,0:T(8,128)(2,1)}, u32[]{:S(2)}) %copy-start) | copy-done | bytes 1835032
  2.2 0.0 copy-start.1
  2.2 1.2 %copy-done.1 = bf16[1,128,4096]{2,1,0:T(8,128)(2,1)S(1)} copy-done((bf16[1,128,4096]{2,1,0:T(8,128)(2,1)S(1)}, bf16[1,128,4096]{2,1,0:T(8,128)(2,1)}, u32[]{:S(2)}) %copy-start.1) | copy-done | bytes 1048600
  3.4 0.0 copy-start.2
  3.4 1.2 %copy-done.2 = bf16[64,7168]{1,0:T(8,128)(2,1)S(1)} copy-done((bf16[64,7168]{1,0:T(8,128)(2,1)S(1)}, bf16[64,7168]{1,0:T(8,128)(2,1)}, u32[]{:S(2)}) %copy-start.2) | copy-done | bytes 917528
  4.6 0.0 copy-start.3
  4.6 1.0 %copy-done.3 = bf16[64,4096]{1,0:T(8,128)(2,1)S(1)} copy-done((bf16[64,4096]{1,0:T(8,128)(2,1)S(1)}, bf16[64,4096]{1,0:T(8,128)(2,1)}, u32[]{:S(2)}) %copy-start.3) | copy-done | bytes 524312
  5.6 0.0 copy-start.4
  5.6 0.8 %copy-done.4 = f32[2,4096]{1,0:T(2,128)S(1)} copy-done((f32[2,4096]{1,0:T(2,128)S(1)}, f32[2,4096]{1,0:T(2,128)}, u32[]{:S(2)}) %copy-start.4) | copy-done | bytes 32792
  6.4 18.0 %shard_map.64 = f32[2,8]{1,0:T(2,128)S(1)} custom-call(s32[1]{0:T(128)S(6)} %copy.8.lengths_ref, f32[2,4096]{1,0:T(2,128)S(1)} %copy-done.4, bf16[1,128,4096]{2,1,0:T(8,128)(2,1)S(1)} %copy-done.1, bf16[1,128,7168]{2,1,0:T(8,128)(2,1)S(1)} %copy-done, bf16[64,4096]{1,0:T(8,128)(2,1)S(1)} %copy-done.3, bf16[64,7168]{1,0:T(8,128)(2,1)S(1)} %copy-done.2), custom_call_target="tpu_custom_call" | custom-call | tf_op jit(solution)/shard_map/pallas_call | solution.py:254
  24.3 0.6 %copy.9 = f32[2,8]{1,0:T(2,128)} copy(f32[2,8]{1,0:T(2,128)S(1)} %shard_map.64) | data formatting | bytes 128
Async XLA Ops:
  0.7 1.5 %copy-start = (bf16[1,128,7168]{2,1,0:T(8,128)(2,1)S(1)}, bf16[1,128,7168]{2,1,0:T(8,128)(2,1)}, u32[]{:S(2)}) copy-start(bf16[1,128,7168]{2,1,0:T(8,128)(2,1)} %xout_hbm.1) | copy-start | bytes 5505028
  2.2 1.2 %copy-start.1 = (bf16[1,128,4096]{2,1,0:T(8,128)(2,1)S(1)}, bf16[1,128,4096]{2,1,0:T(8,128)(2,1)}, u32[]{:S(2)}) copy-start(bf16[1,128,4096]{2,1,0:T(8,128)(2,1)} %xin_hbm.1) | copy-start | bytes 3145732
  3.4 1.2 %copy-start.2 = (bf16[64,7168]{1,0:T(8,128)(2,1)S(1)}, bf16[64,7168]{1,0:T(8,128)(2,1)}, u32[]{:S(2)}) copy-start(bf16[64,7168]{1,0:T(8,128)(2,1)} %pout_hbm.1) | copy-start | bytes 2752516
  4.6 1.0 %copy-start.3 = (bf16[64,4096]{1,0:T(8,128)(2,1)S(1)}, bf16[64,4096]{1,0:T(8,128)(2,1)}, u32[]{:S(2)}) copy-start(bf16[64,4096]{1,0:T(8,128)(2,1)} %pin_hbm.1) | copy-start | bytes 1572868
  5.6 0.8 %copy-start.4 = (f32[2,4096]{1,0:T(2,128)S(1)}, f32[2,4096]{1,0:T(2,128)}, u32[]{:S(2)}) copy-start(f32[2,4096]{1,0:T(2,128)} %tests_ref.1) | copy-start | bytes 98308

commit v2 on v1

--- a/solution.py
+++ b/solution.py
@@ -65,9 +65,9 @@
 
 def kernel(
     n_dp, n_test,
-    lengths_ref, tests_ref, xin_hbm, xout_hbm, pin_hbm, pout_hbm, out_ref,
-    xin, xout, pin, pout, gram, sbuf, xbuf, zbuf, gbuf, tmat, inv_own, inv_other,
-    load_sem, s_send, s_recv, x_send, x_recv, z_send, z_recv, g_send, g_recv, i_send, i_recv,
+    lengths_ref, tests_hbm, xin_hbm, xout_hbm, pin_hbm, pout_hbm, out_ref,
+    tests_ref, xin, xout, pin, pout, gram, sbuf, xbuf, zbuf, gbuf, tmat, inv_own, inv_other,
+    load_sem, small_sem, s_send, s_recv, x_send, x_recv, z_send, z_recv, g_send, g_recv, i_send, i_recv,
 ):
     dp = lax.axis_index("dp")
     test = lax.axis_index("test")
@@ -107,11 +107,8 @@
             steps.append((start, size, both))
         plan.append((x, p, steps))
 
-    for j in range(test_local):
-        for q in range(width * width // wide):
-            piece = tests_ref[j : j + 1, q * wide : (q + 1) * wide]
-            tmat[j, 2 * q : 2 * q + 1, :] = piece
-            tmat[j, 2 * q + 1 : 2 * q + 2, :] = pltpu.roll(piece, width, 1)
+    tests_copy = pltpu.make_async_copy(tests_hbm, tests_ref, small_sem)
+    tests_copy.start()
 
     length = lengths_ref[0]
     slots = core * half_len + lax.broadcasted_iota(jnp.int32, (1, half_len), 1)
@@ -183,6 +180,13 @@
         amount = amount + xbuf[i, width : width + 8, :]
     gbuf[dp, pairs * width : pairs * width + 8, :] = amount
     g_arrivals = spread(gbuf, dp, "dp", n_dp, g_send, g_recv)
+
+    tests_copy.wait()
+    for j in range(test_local):
+        for q in range(width * width // wide):
+            piece = tests_ref[j : j + 1, q * wide : (q + 1) * wide]
+            tmat[j, 2 * q : 2 * q + 1, :] = piece
+            tmat[j, 2 * q + 1 : 2 * q + 2, :] = pltpu.roll(piece, width, 1)
 
     for arrival in z_arrivals:
         arrival.wait_recv()
@@ -249,18 +253,18 @@
     test_local = test_grads.shape[0]
     bf16 = train_inputs.dtype
     n_loads = 2 * (depth_in // chunk_of(depth_in) + depth_out // chunk_of(depth_out))
-    any_space = pl.BlockSpec(memory_space=pl.ANY)
+    any_space = pl.BlockSpec(memory_space=pltpu.HBM)
     dma = pltpu.SemaphoreType.DMA
     return pl.pallas_call(
         functools.partial(kernel, n_dp, n_test),
         out_shape=jax.ShapeDtypeStruct((test_local, n_dp * n_test), F32),
         in_specs=[
             pl.BlockSpec(memory_space=pltpu.SMEM),
-            pl.BlockSpec(memory_space=pltpu.VMEM),
-            any_space, any_space, any_space, any_space,
+            any_space, any_space, any_space, any_space, any_space,
         ],
         out_specs=pl.BlockSpec(memory_space=pltpu.VMEM),
         scratch_shapes=[
+            pltpu.VMEM(test_grads.shape, F32),
             pltpu.VMEM((half_len, depth_in), bf16),
             pltpu.VMEM((half_len, depth_out), bf16),
             pltpu.VMEM((width, depth_in), bf16),
@@ -274,6 +278,7 @@
             pltpu.VMEM((width, wide), F32),
             pltpu.VMEM((width, wide), F32),
             dma((n_loads,)),
+            dma,
             dma, dma,
             dma((n_test - 1,)), dma((n_test - 1,)),
             dma((n_dp - 1,)), dma((n_dp - 1,)),
@@ -281,7 +286,7 @@
             dma, dma,
         ],
         compiler_params=pltpu.CompilerParams(
-            collective_id=0, has_side_effects=True, vmem_limit_bytes=32 * 1024 * 1024
+            collective_id=0, has_side_effects=True, vmem_limit_bytes=60 * 1024 * 1024
         ),
     )(lengths, test_grads, train_inputs, train_grads, proj_in, proj_out)
 

time: 25.2 us -> 21.2 us (0.84)
  local copies, waits for them, and re-layouts: 6.26 us -> 1.24 us
  Pallas kernels: 18 us -> 19.2 us
    unnamed x11 -> x1, local copies, waits for them, and re-layouts: 6.26 us -> 1.24 us
    pallas_call x1, Pallas kernels: 18 us -> 19.2 us  [per_device(): pl.pallas_call(functools.partial(kernel, n_dp, n_test), out_shape=jax.Sha...]
where the time goes in v2:
time: 21.2 us; the launch traced here: 21.1 us
  Pallas kernels  19.2 us (91%)
  local copies, waits for them, and re-layouts  1.24 us (6%)
  between operations  0.66 us (3%)
    pallas_call x1, Pallas kernels, per_device(): pl.pallas_call(functools.partial(kernel, n_dp, n_test), out_shape=jax.Sha...  19.2 us
    unnamed x1, local copies, waits for them, and re-layouts  1.24 us

profile of v2, /device:TPU:1, one launch (start us, length us, event | category | flops | bytes accessed | tf_op | source)
XLA Modules:
  0.0 21.1 jit_solution(16567483207350666370)
XLA Ops:
  0.7 19.2 %shard_map.64 = f32[2,8]{1,0:T(2,128)} custom-call(s32[1]{0:T(128)S(6)} %copy.8.lengths_ref, f32[2,4096]{1,0:T(2,128)} %tests_hbm.1, bf16[1,128,4096]{2,1,0:T(8,128)(2,1)} %xin_hbm.1, bf16[1,128,7168]{2,1,0:T(8,128)(2,1)} %xout_hbm.1, bf16[64,4096]{1,0:T(8,128)(2,1)} %pin_hbm.1, bf16[64,7168]{1,0:T(8,128)(2,1)} %pout_hbm.1), custom_call_target="tpu_custom_call" | custom-call | tf_op jit(solution)/shard_map/pallas_call | solution.py:258
  19.8 1.2 %copy.9 = f32[2,8]{1,0:T(2,128)} copy(f32[2,8]{1,0:T(2,128)} %shard_map.64) | data formatting | bytes 128

commit v3 on v2

--- a/solution.py
+++ b/solution.py
@@ -65,8 +65,8 @@
 
 def kernel(
     n_dp, n_test,
-    lengths_ref, tests_hbm, xin_hbm, xout_hbm, pin_hbm, pout_hbm, out_ref,
-    tests_ref, xin, xout, pin, pout, gram, sbuf, xbuf, zbuf, gbuf, tmat, inv_own, inv_other,
+    lengths_hbm, tests_hbm, xin_hbm, xout_hbm, pin_hbm, pout_hbm, out_ref,
+    lengths_ref, tests_ref, xin, xout, pin, pout, gram, sbuf, xbuf, zbuf, gbuf, tmat, inv_own, inv_other,
     load_sem, small_sem, s_send, s_recv, x_send, x_recv, z_send, z_recv, g_send, g_recv, i_send, i_recv,
 ):
     dp = lax.axis_index("dp")
@@ -107,10 +107,13 @@
             steps.append((start, size, both))
         plan.append((x, p, steps))
 
-    tests_copy = pltpu.make_async_copy(tests_hbm, tests_ref, small_sem)
+    length_copy = pltpu.make_async_copy(lengths_hbm, lengths_ref, small_sem.at[0])
+    length_copy.start()
+    tests_copy = pltpu.make_async_copy(tests_hbm, tests_ref, small_sem.at[1])
     tests_copy.start()
 
-    length = lengths_ref[0]
+    length_copy.wait()
+    length = lengths_ref[...]
     slots = core * half_len + lax.broadcasted_iota(jnp.int32, (1, half_len), 1)
     valid = (slots < length).astype(F32)
     lows = []
@@ -135,7 +138,7 @@
     s_copy.start()
     mine = dot_nt(own, jnp.concatenate([own, oth], axis=0), HIGHEST)
     tokens = jnp.clip(length, 0, 2 * half_len).astype(F32)
-    xbuf[test, width : width + 8, :] = jnp.full((8, wide), tokens, F32)
+    xbuf[test, width : width + 8, :] = jnp.broadcast_to(tokens, (8, wide))
     s_copy.wait_recv()
     xbuf[test, 0:width, :] = mine + sbuf[...]
 
@@ -259,11 +262,11 @@
         functools.partial(kernel, n_dp, n_test),
         out_shape=jax.ShapeDtypeStruct((test_local, n_dp * n_test), F32),
         in_specs=[
-            pl.BlockSpec(memory_space=pltpu.SMEM),
-            any_space, any_space, any_space, any_space, any_space,
+            any_space, any_space, any_space, any_space, any_space, any_space,
         ],
         out_specs=pl.BlockSpec(memory_space=pltpu.VMEM),
         scratch_shapes=[
+            pltpu.VMEM((1, 1), jnp.int32),
             pltpu.VMEM(test_grads.shape, F32),
             pltpu.VMEM((half_len, depth_in), bf16),
             pltpu.VMEM((half_len, depth_out), bf16),
@@ -278,7 +281,7 @@
             pltpu.VMEM((width, wide), F32),
             pltpu.VMEM((width, wide), F32),
             dma((n_loads,)),
-            dma,
+            dma((2,)),
             dma, dma,
             dma((n_test - 1,)), dma((n_test - 1,)),
             dma((n_dp - 1,)), dma((n_dp - 1,)),
@@ -286,9 +289,9 @@
             dma, dma,
         ],
         compiler_params=pltpu.CompilerParams(
-            collective_id=0, has_side_effects=True, vmem_limit_bytes=60 * 1024 * 1024
+            collective_id=0, has_side_effects=True, vmem_limit_bytes=55200 * 1024
         ),
-    )(lengths, test_grads, train_inputs, train_grads, proj_in, proj_out)
+    )(lengths.reshape(1, 1), test_grads, train_inputs, train_grads, proj_in, proj_out)
 
 
 def solution(mesh):

time: 21.2 us -> 20 us (0.943)
  local copies, waits for them, and re-layouts: 1.24 us -> 0.56 us
  Pallas kernels: 19.2 us -> 18.6 us
    unnamed x1, local copies, waits for them, and re-layouts: 1.24 us -> 0.56 us
    pallas_call x1, Pallas kernels: 19.2 us -> 18.6 us  [per_device(): pl.pallas_call(functools.partial(kernel, n_dp, n_test), out_shape=jax.Sha...]
where the time goes in v3:
time: 20 us; the launch traced here: 19.8 us
  Pallas kernels  18.6 us (93%)
  between operations  0.66 us (3%)
  local copies, waits for them, and re-layouts  0.56 us (3%)
    pallas_call x1, Pallas kernels, per_device(): pl.pallas_call(functools.partial(kernel, n_dp, n_test), out_shape=jax.Sha...  18.6 us
    unnamed x1, local copies, waits for them, and re-layouts  0.56 us

profile of v3, /device:TPU:1, one launch (start us, length us, event | category | flops | bytes accessed | tf_op | source)
XLA Modules:
  0.0 19.8 jit_solution(1458653149868451942)
XLA Ops:
  0.7 18.6 %shard_map.64 = f32[2,8]{1,0:T(2,128)S(1)} custom-call(s32[1,1]{1,0:T(1,128)} %bitcast.1.lengths_hbm, f32[2,4096]{1,0:T(2,128)} %tests_hbm.1, bf16[1,128,4096]{2,1,0:T(8,128)(2,1)} %xin_hbm.1, bf16[1,128,7168]{2,1,0:T(8,128)(2,1)} %xout_hbm.1, bf16[64,4096]{1,0:T(8,128)(2,1)} %pin_hbm.1, bf16[64,7168]{1,0:T(8,128)(2,1)} %pout_hbm.1), custom_call_target="tpu_custom_call" | custom-call | tf_op jit(solution)/shard_map/pallas_call | solution.py:261
  19.2 0.6 %copy.9 = f32[2,8]{1,0:T(2,128)} copy(f32[2,8]{1,0:T(2,128)S(1)} %shard_map.64) | data formatting | bytes 128

commit v4 on v3

--- a/solution.py
+++ b/solution.py
@@ -66,8 +66,8 @@
 def kernel(
     n_dp, n_test,
     lengths_hbm, tests_hbm, xin_hbm, xout_hbm, pin_hbm, pout_hbm, out_ref,
-    lengths_ref, tests_ref, xin, xout, pin, pout, gram, sbuf, xbuf, zbuf, gbuf, tmat, inv_own, inv_other,
-    load_sem, small_sem, s_send, s_recv, x_send, x_recv, z_send, z_recv, g_send, g_recv, i_send, i_recv,
+    lengths_ref, tests_ref, xin, xout, pin, pout, obuf, ebuf, sbuf, pbuf, zbuf, gbuf, tmat, inv_own, inv_other,
+    load_sem, small_sem, p_send, p_recv, s_send, s_recv, x_send, x_recv, z_send, z_recv, g_send, g_recv, i_send, i_recv,
 ):
     dp = lax.axis_index("dp")
     test = lax.axis_index("test")
@@ -78,10 +78,11 @@
     test_local = tests_ref.shape[0]
     wide = 2 * width
     half = width // 2
-    pairs = n_test // 2
 
     partners = [{"seq": 1 - core}]
-    partners += [{"test": lax.rem(test + d, n_test)} for d in range(1, n_test)]
+    for d in range(1, n_test):
+        partners.append({"test": lax.rem(test + d, n_test)})
+        partners.append({"test": lax.rem(test + d, n_test), "seq": 1 - core})
     partners += [{"dp": lax.rem(dp + d, n_dp)} for d in range(1, n_dp)]
 
     barrier = pltpu.get_barrier_semaphore()
@@ -130,59 +131,91 @@
 
     pl.semaphore_wait(barrier, len(partners))
 
-    gram[...] = dot_nt(oth, jnp.concatenate([oth, own], axis=0), HIGHEST)
-    s_copy = pltpu.make_async_remote_copy(
-        gram, sbuf, s_send, s_recv, device_id={"seq": 1 - core},
-        device_id_type=pl.DeviceIdType.MESH,
-    )
-    s_copy.start()
-    mine = dot_nt(own, jnp.concatenate([own, oth], axis=0), HIGHEST)
-    tokens = jnp.clip(length, 0, 2 * half_len).astype(F32)
-    xbuf[test, width : width + 8, :] = jnp.broadcast_to(tokens, (8, wide))
-    s_copy.wait_recv()
-    xbuf[test, 0:width, :] = mine + sbuf[...]
-
-    waits = [s_copy]
-
-    def spread(buffer, me, axis, n, send, recv):
-        arrivals = []
-        for d in range(1, n):
-            copy = pltpu.make_async_remote_copy(
-                buffer.at[me], buffer.at[me], send.at[d - 1], recv.at[d - 1],
-                device_id={axis: lax.rem(me + d, n)}, device_id_type=pl.DeviceIdType.MESH,
-            )
+    left = lax.broadcasted_iota(jnp.int32, (half, wide), 1) < width
+
+    def twice(a, b):
+        return dot_nt(a, jnp.concatenate([b, b], axis=0), HIGHEST)
+
+    def pack(twin):
+        return jnp.where(left, twin[0:half], twin[half:width])
+
+    waits = []
+
+    def remote(src, dst, send, recv, where, start=True):
+        copy = pltpu.make_async_remote_copy(
+            src, dst, send, recv, device_id=where, device_id_type=pl.DeviceIdType.MESH
+        )
+        if start:
             copy.start()
             waits.append(copy)
-            source = lax.rem(me + n - d, n)
-            arrivals.append(
-                pltpu.make_async_remote_copy(
-                    buffer.at[source], buffer.at[source], send.at[d - 1], recv.at[d - 1],
-                    device_id={axis: lax.rem(me + d, n)}, device_id_type=pl.DeviceIdType.MESH,
-                )
-            )
-        return arrivals
-
-    for arrival in spread(xbuf, test, "test", n_test, x_send, x_recv):
+        return copy
+
+    other = 1 - core
+    obuf[...] = pack(twice(oth, oth))
+    part_arrivals = []
+
+    def send_part(d, flip):
+        to = lax.rem(test + d, n_test)
+        source = lax.rem(test + n_test - d, n_test)
+        where = {"test": to, "seq": other if flip else core}
+        slot = pbuf.at[core, test]
+        sems = (p_send.at[flip, d], p_recv.at[flip, d])
+        remote(obuf if flip else slot, slot, *sems, where)
+        arrived = pbuf.at[other if flip else core, source]
+        part_arrivals.append(remote(arrived, arrived, *sems, where, start=False))
+
+    for d in range(n_test - 1, -1, -1):
+        send_part(d, 1)
+    pbuf[core, test] = pack(twice(own, own))
+    for d in range(n_test - 1, 0, -1):
+        send_part(d, 0)
+
+    ebuf[...] = pack(twice(oth, own))
+    e_copy = remote(ebuf, sbuf, s_send, s_recv, {"seq": other})
+    cross = pack(twice(own, oth))
+    tokens = jnp.clip(length, 0, 2 * half_len).astype(F32)
+    gbuf[dp, test, half : half + 8, :] = jnp.broadcast_to(tokens, (8, wide))
+    e_copy.wait_recv()
+    gbuf[dp, test, 0:half, :] = cross + sbuf[...]
+
+    test_arrivals = []
+    for d in range(1, n_test):
+        where = {"test": lax.rem(test + d, n_test)}
+        sems = (x_send.at[d - 1], x_recv.at[d - 1])
+        remote(gbuf.at[dp, test], gbuf.at[dp, test], *sems, where)
+        arrived = gbuf.at[dp, lax.rem(test + n_test - d, n_test)]
+        test_arrivals.append(remote(arrived, arrived, *sems, where, start=False))
+    g_arrivals = []
+
+    def send_along(t, d):
+        at = lax.rem(test + n_test - t, n_test)
+        where = {"dp": lax.rem(dp + d, n_dp)}
+        sems = (g_send.at[t, d - 1], g_recv.at[t, d - 1])
+        remote(gbuf.at[dp, at], gbuf.at[dp, at], *sems, where)
+        arrived = gbuf.at[lax.rem(dp + n_dp - d, n_dp), at]
+        g_arrivals.append(remote(arrived, arrived, *sems, where, start=False))
+
+    for d in range(1, n_dp):
+        send_along(0, d)
+
+    for arrival in part_arrivals:
         arrival.wait_recv()
-    lane = lax.broadcasted_iota(jnp.int32, (half, wide), 1)
-    left = lane < width
-    cov = xbuf[0, 0:width, :]
-    for i in range(1, n_test):
-        cov = cov + xbuf[i, 0:width, :]
-    zbuf[dp] = jnp.where(left, cov[0:half], pltpu.roll(cov[half:width], width, 1))
-    z_arrivals = spread(zbuf, dp, "dp", n_dp, z_send, z_recv)
-    left_full = lax.broadcasted_iota(jnp.int32, (width, wide), 1) < width
-    for i in range(pairs):
-        gbuf[dp, i * width : (i + 1) * width, :] = jnp.where(
-            left_full,
-            pltpu.roll(xbuf[2 * i, 0:width, :], width, 1),
-            xbuf[2 * i + 1, 0:width, :],
-        )
-    amount = xbuf[0, width : width + 8, :]
-    for i in range(1, n_test):
-        amount = amount + xbuf[i, width : width + 8, :]
-    gbuf[dp, pairs * width : pairs * width + 8, :] = amount
-    g_arrivals = spread(gbuf, dp, "dp", n_dp, g_send, g_recv)
+    cov = None
+    for c in range(2):
+        for t in range(n_test):
+            cov = pbuf[c, t] if cov is None else cov + pbuf[c, t]
+    zbuf[dp] = cov
+    z_arrivals = []
+    for d in range(1, n_dp):
+        where = {"dp": lax.rem(dp + d, n_dp)}
+        sems = (z_send.at[d - 1], z_recv.at[d - 1])
+        remote(zbuf.at[dp], zbuf.at[dp], *sems, where)
+        arrived = zbuf.at[lax.rem(dp + n_dp - d, n_dp)]
+        z_arrivals.append(remote(arrived, arrived, *sems, where, start=False))
+    for t in range(1, n_test):
+        test_arrivals[t - 1].wait_recv()
+        for d in range(1, n_dp):
+            send_along(t, d)
 
     tests_copy.wait()
     for j in range(test_local):
@@ -209,12 +242,7 @@
     tiles = twin_inverse([damped[8 * i : 8 * i + 8] for i in range(width // 8)], width)
     inverse = jnp.concatenate(tiles, axis=0)
     inv_own[...] = inverse
-    i_copy = pltpu.make_async_remote_copy(
-        inv_own, inv_other, i_send, i_recv, device_id={"seq": 1 - core},
-        device_id_type=pl.DeviceIdType.MESH,
-    )
-    i_copy.start()
-    waits.append(i_copy)
+    i_copy = remote(inv_own, inv_other, i_send, i_recv, {"seq": other})
 
     sides = []
     for j in range(test_local):
@@ -223,24 +251,21 @@
     sides = jnp.concatenate(sides, axis=0)
     for arrival in g_arrivals:
         arrival.wait_recv()
-    amount = gbuf[0, pairs * width : pairs * width + 1, :]
-    for i in range(1, n_dp):
-        amount = amount + gbuf[i, pairs * width : pairs * width + 1, :]
+    amount = None
+    for z in range(n_dp):
+        for t in range(n_test):
+            more = gbuf[z, t, half : half + 1, :]
+            amount = more if amount is None else amount + more
+    amount = amount * amount
     i_copy.wait_recv()
     scorer = dot_nn(sides, inv_other[...])
-    left_row = lax.broadcasted_iota(jnp.int32, (1, wide), 1) < width
     ones = jnp.ones((8, wide), F32)
     for j in range(test_local):
+        packed = pack(scorer[j * width : (j + 1) * width])
         rows = []
         for z in range(n_dp):
-            for i in range(pairs):
-                part = jnp.sum(
-                    scorer[j * width : (j + 1) * width] * gbuf[z, i * width : (i + 1) * width, :],
-                    axis=0, keepdims=True,
-                )
-                part = part * amount * amount
-                rows.append(jnp.where(left_row, part, 0.0))
-                rows.append(jnp.where(left_row, 0.0, part))
+            for t in range(n_test):
+                rows.append(jnp.sum(packed * gbuf[z, t, 0:half, :], axis=0, keepdims=True) * amount)
         result = dot_nt(ones, jnp.concatenate(rows, axis=0), HIGHEST)
         out_ref[j : j + 1, :] = result[0:1, :]
 
@@ -252,7 +277,7 @@
     _, half_len, depth_in = train_inputs.shape
     depth_out = train_grads.shape[2]
     width = proj_in.shape[0]
-    wide = 2 * width
+    wide, half = 2 * width, width // 2
     test_local = test_grads.shape[0]
     bf16 = train_inputs.dtype
     n_loads = 2 * (depth_in // chunk_of(depth_in) + depth_out // chunk_of(depth_out))
@@ -272,20 +297,22 @@
             pltpu.VMEM((half_len, depth_out), bf16),
             pltpu.VMEM((width, depth_in), bf16),
             pltpu.VMEM((width, depth_out), bf16),
-            pltpu.VMEM((width, wide), F32),
-            pltpu.VMEM((width, wide), F32),
-            pltpu.VMEM((n_test, width + 8, wide), F32),
-            pltpu.VMEM((n_dp, width // 2, wide), F32),
-            pltpu.VMEM((n_dp, n_test // 2 * width + 8, wide), F32),
+            pltpu.VMEM((half, wide), F32),
+            pltpu.VMEM((half, wide), F32),
+            pltpu.VMEM((half, wide), F32),
+            pltpu.VMEM((2, n_test, half, wide), F32),
+            pltpu.VMEM((n_dp, half, wide), F32),
+            pltpu.VMEM((n_dp, n_test, half + 8, wide), F32),
             pltpu.VMEM((test_local, width, wide), F32),
             pltpu.VMEM((width, wide), F32),
             pltpu.VMEM((width, wide), F32),
             dma((n_loads,)),
             dma((2,)),
+            dma((2, n_test)), dma((2, n_test)),
             dma, dma,
             dma((n_test - 1,)), dma((n_test - 1,)),
             dma((n_dp - 1,)), dma((n_dp - 1,)),
-            dma((n_dp - 1,)), dma((n_dp - 1,)),
+            dma((n_test, n_dp - 1)), dma((n_test, n_dp - 1)),
             dma, dma,
         ],
         compiler_params=pltpu.CompilerParams(

time: 20 us -> 18.7 us (0.935)
  Pallas kernels: 18.6 us -> 17.3 us
    pallas_call x1, Pallas kernels: 18.6 us -> 17.3 us  [per_device(): pl.pallas_call(functools.partial(kernel, n_dp, n_test), out_shape=jax.Sha...]
where the time goes in v4:
time: 18.7 us; the launch traced here: 18.6 us
  Pallas kernels  17.3 us (93%)
  between operations  0.66 us (4%)
  local copies, waits for them, and re-layouts  0.56 us (3%)
    pallas_call x1, Pallas kernels, per_device(): pl.pallas_call(functools.partial(kernel, n_dp, n_test), out_shape=jax.Sha...  17.3 us
    unnamed x1, local copies, waits for them, and re-layouts  0.56 us

profile of v4, /device:TPU:1, one launch (start us, length us, event | category | flops | bytes accessed | tf_op | source)
XLA Modules:
  0.0 18.6 jit_solution(9973251858841843957)
XLA Ops:
  0.7 17.3 %shard_map.64 = f32[2,8]{1,0:T(2,128)S(1)} custom-call(s32[1,1]{1,0:T(1,128)} %bitcast.1.lengths_hbm, f32[2,4096]{1,0:T(2,128)} %tests_hbm.1, bf16[1,128,4096]{2,1,0:T(8,128)(2,1)} %xin_hbm.1, bf16[1,128,7168]{2,1,0:T(8,128)(2,1)} %xout_hbm.1, bf16[64,4096]{1,0:T(8,128)(2,1)} %pin_hbm.1, bf16[64,7168]{1,0:T(8,128)(2,1)} %pout_hbm.1), custom_call_target="tpu_custom_call" | custom-call | tf_op jit(solution)/shard_map/pallas_call | solution.py:286
  18.0 0.6 %copy.9 = f32[2,8]{1,0:T(2,128)} copy(f32[2,8]{1,0:T(2,128)S(1)} %shard_map.64) | data formatting | bytes 128
